TPU v7x, 128 devices: a whole 4x4x4 slice. The times are simulated.
128 devices in a mesh: dp: 4 (over x), expert: 32 (over y, z, core).
Axes of the slice: x: 4, y: 4, z: 4, core: 2. Of those that a mesh axis runs over, the one named last changes fastest.
Arguments:
- tokens: bfloat16 [8192, 7168], P('expert', 'dp'), may hold values from -6 to 6
- cotangent: bfloat16 [8192, 7168], P('expert', 'dp'), may hold values from -6 to 6
- expert_ids: int32 [8192, 8], P('expert'), may hold values from 0 to 255, all different within a row; in each aligned block of 256 rows (0 to 255, 256 to 511, ...) at most 16 rows name the same one
- gate_coef: bfloat16 [8192, 8], P('expert'), may hold values from 0.049804688 to 0.5
- w_gate: bfloat16 [32, 7168, 1024], P('expert', 'dp'), may hold values from -0.0625 to 0.0625
- w_up: bfloat16 [32, 7168, 1024], P('expert', 'dp'), may hold values from -0.0625 to 0.0625
- w_down: bfloat16 [32, 1024, 7168], P('expert', None, 'dp'), may hold values from -0.1875 to 0.1875
Outputs:
- grad_tokens: bfloat16 [8192, 7168], P('expert', 'dp')
- grad_gate: bfloat16 [32, 7168, 1024], P('expert', 'dp')
- grad_up: bfloat16 [32, 7168, 1024], P('expert', 'dp')
- grad_down: bfloat16 [32, 1024, 7168], P('expert', None, 'dp')
Inputs may be any that keep to these rules, and one draw needn't show every extreme that they name: `expert_ids`: each row names 8 different experts; the rows of one index of expert (aligned blocks of 256 rows) name any one expert at most 16 times, a bound that some block reaches.
All inputs are finite; a program needn't handle non-finite values.
Results may differ from a plain program's by a relative error of at most 0.022.
Values may be sent and summed in bfloat16 or wider, within the bound.
A program may use at most 128 MiB of HBM per device.

v0:
```python
import jax
import jax.numpy as jnp
from jax import lax
from jax.sharding import PartitionSpec as P


def gate_parts(gate_pre):
    squash = jax.nn.sigmoid(gate_pre)
    return (squash, gate_pre * squash)


def local(tokens, cotangent, expert_ids, gate_coef, w_gate, w_up, w_down):
    tok_rows, quarter = tokens.shape
    picks_per = expert_ids.shape[1]
    experts = lax.axis_size("expert")
    capacity = 2 * tok_rows * picks_per // (8 * experts)
    slot_count = experts * capacity
    pick_count = tok_rows * picks_per
    flat_ids = expert_ids.reshape(pick_count)
    inside = flat_ids < experts
    onehot = (
        (flat_ids[:, None] == jnp.arange(experts, dtype=jnp.int32)[None, :]) & inside[:, None]
    ).astype(jnp.int32)
    before = jnp.cumsum(onehot, axis=0) - onehot
    within = jnp.sum(before * onehot, axis=1)
    target = jnp.where(inside, flat_ids * capacity + within, slot_count)
    holder = (
        jnp.zeros((slot_count,), jnp.int32)
        .at[target]
        .set(jnp.arange(1, pick_count + 1, dtype=jnp.int32), mode="drop")
    )
    filled = holder > 0
    source = jnp.maximum(holder - 1, 0)
    token_of = source // picks_per
    empty_value = jnp.zeros((), jnp.bfloat16)
    sent_rows = jnp.where(filled[:, None], tokens[token_of], empty_value).reshape(
        experts, capacity, quarter
    )
    sent_cot = jnp.where(filled[:, None], cotangent[token_of], empty_value).reshape(
        experts, capacity, quarter
    )
    sent_coef = jnp.where(filled, gate_coef.reshape(pick_count)[source], empty_value).reshape(
        experts, capacity
    )
    rows_in, cot_in, coef_in = (
        lax.all_to_all(sent_rows, "expert", split_axis=0, concat_axis=0, tiled=True),
        lax.all_to_all(sent_cot, "expert", split_axis=0, concat_axis=0, tiled=True),
        lax.all_to_all(sent_coef, "expert", split_axis=0, concat_axis=0, tiled=True),
    )
    slot_rows = rows_in.reshape(slot_count, quarter)
    cot_rows = cot_in.reshape(slot_count, quarter)
    coef_rows = coef_in.reshape(slot_count)
    gate_mat = w_gate[0]
    up_mat = w_up[0]
    down_mat = w_down[0]
    gate_part = jnp.dot(slot_rows, gate_mat, preferred_element_type=jnp.float32)
    up_part = jnp.dot(slot_rows, up_mat, preferred_element_type=jnp.float32)
    scaled = (coef_rows.astype(jnp.float32)[:, None] * cot_rows.astype(jnp.float32)).astype(
        jnp.bfloat16
    )
    back_part = lax.dot_general(
        scaled, down_mat, (((1,), (1,)), ((), ())), preferred_element_type=jnp.float32
    )
    gate_pre, up_pre, grad_hidden = (
        lax.psum(gate_part.astype(jnp.bfloat16), "dp").astype(jnp.float32),
        lax.psum(up_part.astype(jnp.bfloat16), "dp").astype(jnp.float32),
        lax.psum(back_part.astype(jnp.bfloat16), "dp").astype(jnp.float32),
    )
    squash, silu_out = gate_parts(gate_pre)
    hidden = (silu_out * up_pre).astype(jnp.bfloat16)
    back_gate = (grad_hidden * up_pre * squash * (1.0 + gate_pre * (1.0 - squash))).astype(
        jnp.bfloat16
    )
    back_up = (grad_hidden * silu_out).astype(jnp.bfloat16)
    grad_down = lax.dot_general(
        hidden, scaled, (((0,), (0,)), ((), ())), preferred_element_type=jnp.float32
    ).astype(jnp.bfloat16)
    grad_gate = lax.dot_general(
        slot_rows, back_gate, (((0,), (0,)), ((), ())), preferred_element_type=jnp.float32
    ).astype(jnp.bfloat16)
    grad_up = lax.dot_general(
        slot_rows, back_up, (((0,), (0,)), ((), ())), preferred_element_type=jnp.float32
    ).astype(jnp.bfloat16)
    contrib = lax.dot_general(
        back_gate, gate_mat, (((1,), (1,)), ((), ())), preferred_element_type=jnp.float32
    )
    contrib = contrib + lax.dot_general(
        back_up, up_mat, (((1,), (1,)), ((), ())), preferred_element_type=jnp.float32
    )
    contrib = contrib.astype(jnp.bfloat16).reshape(experts, capacity, quarter)
    returned = lax.all_to_all(contrib, "expert", split_axis=0, concat_axis=0, tiled=True).reshape(
        slot_count, quarter
    )
    per_pick = returned[jnp.minimum(target, slot_count - 1)]
    per_pick = jnp.where(inside[:, None], per_pick, empty_value).reshape(
        tok_rows, picks_per, quarter
    )
    summed = jnp.sum(per_pick, axis=1, dtype=jnp.float32)
    return (summed.astype(jnp.bfloat16), grad_gate[None], grad_up[None], grad_down[None])


def solution(mesh):
    in_specs = (
        P("expert", "dp"),
        P("expert", "dp"),
        P("expert", None),
        P("expert", None),
        P("expert", "dp", None),
        P("expert", "dp", None),
        P("expert", None, "dp"),
    )
    out_specs = (
        P("expert", "dp"),
        P("expert", "dp", None),
        P("expert", "dp", None),
        P("expert", None, "dp"),
    )
    return jax.shard_map(local, mesh=mesh, in_specs=in_specs, out_specs=out_specs, check_vma=False)
```

profile of v0, /device:TPU:1, one launch (start us, length us, event | category | flops | bytes accessed | tf_op | source)
XLA Modules:
  0.0 261.6 jit_solution(7354473828410790250)
XLA Ops:
  7.2 0.8 broadcast_compare_fusion.2
  8.0 0.7 broadcast_multiply_fusion
  8.7 0.8 copy.23
  9.5 0.1 eq.29
  9.6 0.1 eq.25
  9.7 0.2 copy.20
  9.9 0.1 lt.60
  10.0 0.1 copy.22
  10.2 0.1 mul.59
  10.3 9.1 %reduce-window.6 = s32[32,16,128]{2,1,0:T(8,128)S(1)} reduce-window(s32[32,16,128]{2,1,0:T(8,128)S(1)} %fusion.41, s32[]{:T(128)} %constant.18.clone.1), window={size=1x1x128 pad=0_0x0_0x127_0}, to_apply=%region_0.0 | reduce-window | flops 8323072 | bytes 524292 | tf_op jit(solution)/shard_map/reduce-window
  19.4 0.1 slice.16
  19.6 0.2 copy.29
  19.8 0.2 reduce-window.9
  20.0 0.1 broadcast_add_fusion
  20.1 0.1 fusion.38
  20.3 8.0 %scatter_custom_fusion = s32[512]{0:T(512)S(1)} fusion(s32[2048]{0:T(1024)S(1)} %bitcast.86, s32[2048]{0:T(1024)S(1)} %iota_add_fusion, s32[]{:T(128)} %constant.18.clone.1), kind=kCustom, calls=%fused_computation.75 | custom fusion | bytes 2052 | tf_op jit(solution)/shard_map/scatter | solution.py:30
  28.4 0.1 copy.27
  28.5 0.1 reshape.159
  28.6 3.5 %gather_fusion = bf16[512]{0:T(512)(128)(2,1)S(1)} fusion(bf16[2048]{0:T(1024)(128)(2,1)S(1)} %reshape.159, s32[1024]{0:T(1024)S(1)} %get-tuple-element.16), kind=kCustom, calls=%fused_computation | custom fusion | bytes 4096 | tf_op jit(solution)/shard_map/gather | solution.py:42
  32.2 0.7 all_to_all.20
  32.9 9.6 %all-to-all-start = ((bf16[32,1,16]{2,1,0:T(2,128)(2,1)}), bf16[32,1,16]{2,1,0:T(2,128)(2,1)S(1)}, u32[]{:S(2)}, u32[]{:S(2)}) async-start(bf16[32,1,16]{2,1,0:T(2,128)(2,1)} %all_to_all.20), calls=%async_computation | async-start | bytes 32768 | tf_op jit(solution)/shard_map/all_to_all | solution.py:48
  42.5 0.1 broadcast_in_dim.66
  42.6 3.1 %gather_fusion.1 = bf16[512,1792]{1,0:T(8,128)(2,1)} fusion(bf16[256,1792]{1,0:T(8,128)(2,1)S(1)} %copy-done, s32[1024]{0:T(1024)S(1)} %get-tuple-element.15), kind=kCustom, calls=%fused_computation.1 | custom fusion | bytes 3672064 | tf_op jit(solution)/shard_map/gather | solution.py:39
  45.7 3.1 %gather_fusion.2 = bf16[512,1792]{1,0:T(8,128)(2,1)} fusion(bf16[256,1792]{1,0:T(8,128)(2,1)S(1)} %copy-done.1, s32[1024]{0:T(1024)S(1)} %get-tuple-element.15), kind=kCustom, calls=%fused_computation.2 | custom fusion | bytes 3672064 | tf_op jit(solution)/shard_map/gather | solution.py:36
  48.8 3.6 %broadcast_select_fusion.1 = (bf16[32,16,1792]{2,1,0:T(8,128)(2,1)}, bf16[32,16,1792]{2,1,0:T(8,128)(2,1)S(1)}) fusion(bf16[32,16,1792]{2,1,0:T(8,128)(2,1)} %bitcast.72, pred[32,16]{1,0:T(8,128)(4,1)S(1)} %broadcast_in_dim.66, bf16[32,16,1792]{2,1,0:T(8,128)(2,1)} %bitcast.73), kind=kLoop, calls=%fused_computation.43 | loop fusion | flops 1835008 | bytes 7340544 | tf_op jit(solution)/shard_map/jit(_where)/select_n | solution.py:39
  52.4 32.7 %all_to_all.25 = bf16[32,16,1792]{2,1,0:T(8,128)(2,1)} all-to-all(bf16[32,16,1792]{2,1,0:T(8,128)(2,1)S(1)} %get-tuple-element.12), channel_id=1, replica_groups=mesh['dp'=4,'expert'=32] {'expert'}, dimensions={0} | all-to-all | bytes 3670016 | tf_op jit(solution)/shard_map/all_to_all | solution.py:46
  85.2 3.8 %all-to-all-start.1 = ((bf16[32,16,1792]{2,1,0:T(8,128)(2,1)}), bf16[32,16,1792]{2,1,0:T(8,128)(2,1)S(1)}, u32[]{:S(2)}, u32[]{:S(2)}) async-start(bf16[32,16,1792]{2,1,0:T(8,128)(2,1)} %get-tuple-element.11), calls=%async_computation.1 | async-start | bytes 3670016 | tf_op jit(solution)/shard_map/all_to_all | solution.py:47
  89.0 0.2 all-reduce.3.cloned.1.call-start
  89.3 5.8 %fusion.29 = bf16[512,1024]{1,0:T(8,128)(2,1)} fusion(bf16[512,1792]{1,0:T(8,128)(2,1)} %bitcast.74, bf16[1,1792,1024]{2,1,0:T(8,128)(2,1)} %param.12), kind=kOutput, calls=%fused_computation.45 | convolution fusion | flops 1879572480 | bytes 6553600 | tf_op jit(solution)/shard_map/dot_general | solution.py:57
  95.1 3.0 %fusion.32 = bf16[512,1024]{1,0:T(8,128)(2,1)} fusion(bf16[512,1792]{1,0:T(8,128)(2,1)S(1)} %bitcast.75, bf16[1,1792,1024]{2,1,0:T(8,128)(2,1)S(1)} %copy-done.6), kind=kOutput, calls=%fused_computation.46 | convolution fusion | flops 1879572480 | bytes 6553600 | tf_op jit(solution)/shard_map/dot_general | solution.py:56
  98.1 16.4 %all-to-all-done.1 = bf16[32,16,1792]{2,1,0:T(8,128)(2,1)S(1)} async-done(((bf16[32,16,1792]{2,1,0:T(8,128)(2,1)}), bf16[32,16,1792]{2,1,0:T(8,128)(2,1)S(1)}, u32[]{:S(2)}, u32[]{:S(2)}) %all-to-all-start.1) | async-done | bytes 1835040 | tf_op jit(solution)/shard_map/all_to_all | solution.py:47
  114.5 0.4 multiply_convert_fusion
  114.9 1.7 copy-done.5
  116.6 3.1 %fusion.26 = bf16[512,1024]{1,0:T(8,128)(2,1)} fusion(bf16[512,1792]{1,0:T(8,128)(2,1)S(1)} %bitcast.79, bf16[1,1024,1792]{2,1,0:T(8,128)(2,1)S(1)} %copy-done.5), kind=kOutput, calls=%fused_computation.44 | convolution fusion | flops 1879572480 | bytes 6553600 | tf_op jit(solution)/shard_map/dot_general | solution.py:61
  119.6 0.0 all-reduce.3.cloned.1.call-update
  119.6 0.1 convert_reduce_fusion
  119.7 0.1 reshape.164
  119.8 1.6 fusion.1
  121.4 71.9 %all-reduce.3.cloned.1.call-done = (bf16[512,1024]{1,0:T(8,128)(2,1)}, bf16[512,1024]{1,0:T(8,128)(2,1)}, bf16[512,1024]{1,0:T(8,128)(2,1)}) async-done(((bf16[512,1024]{1,0:T(8,128)(2,1)}, bf16[512,1024]{1,0:T(8,128)(2,1)}, bf16[512,1024]{1,0:T(8,128)(2,1)}), (bf16[512,1024]{1,0:T(8,128)(2,1)}, bf16[512,1024]{1,0:T(8,128)(2,1)}, bf16[512,1024]{1,0:T(8,128)(2,1)})) %all-reduce.3.cloned.1.call-update) | async-done | bytes 3145744 | tf_op jit(solution)/shard_map/psum | solution.py:66
  193.3 5.9 %fusion.2 = f32[512,1792]{1,0:T(8,128)S(1)} fusion(bf16[1,1792,1024]{2,1,0:T(8,128)(2,1)} %param.11, bf16[512,1024]{1,0:T(8,128)(2,1)} %get-tuple-element.4, bf16[512,1024]{1,0:T(8,128)(2,1)} %get-tuple-element.5, bf16[512,1024]{1,0:T(8,128)(2,1)} %get-tuple-element.6), kind=kOutput, calls=%fused_computation.12 | convolution fusion | flops 1885863936 | bytes 10485760 | tf_op jit(solution)/shard_map/dot_general | solution.py:84
  199.3 3.8 %add_convert_fusion = bf16[512,1792]{1,0:T(8,128)(2,1)} fusion(f32[512,1792]{1,0:T(8,128)S(1)} %fusion.2, bf16[1,1792,1024]{2,1,0:T(8,128)(2,1)S(1)} %copy-done.7, bf16[512,1024]{1,0:T(8,128)(2,1)S(1)} %copy-done.9, bf16[512,1024]{1,0:T(8,128)(2,1)S(1)} %copy-done.11), kind=kOutput, calls=%fused_computation.22 | convolution fusion | flops 1885077504 | bytes 11272192 | tf_op jit(solution)/shard_map/dot_general | solution.py:87
  203.0 7.7 %all-to-all-start.3 = ((bf16[32,16,1792]{2,1,0:T(8,128)(2,1)}), bf16[32,16,1792]{2,1,0:T(8,128)(2,1)S(1)}, u32[]{:S(2)}, u32[]{:S(2)}) async-start(bf16[32,16,1792]{2,1,0:T(8,128)(2,1)} %bitcast.78), calls=%async_computation.3 | async-start | bytes 3670016 | tf_op jit(solution)/shard_map/all_to_all | solution.py:91
  210.8 6.4 %fusion.14 = bf16[1,1024,1792]{2,1,0:T(8,128)(2,1)} fusion(bf16[512,1792]{1,0:T(8,128)(2,1)} %fusion.1, bf16[512,1024]{1,0:T(8,128)(2,1)} %get-tuple-element.4, bf16[512,1024]{1,0:T(8,128)(2,1)} %get-tuple-element.6), kind=kOutput, calls=%fused_computation.26 | convolution fusion | flops 1885077504 | bytes 7602176 | tf_op jit(solution)/shard_map/dot_general | solution.py:75
  217.2 4.1 %fusion.13 = bf16[1,1792,1024]{2,1,0:T(8,128)(2,1)} fusion(bf16[512,1792]{1,0:T(8,128)(2,1)S(1)} %bitcast.76, bf16[512,1024]{1,0:T(8,128)(2,1)S(1)} %copy-done.10, bf16[512,1024]{1,0:T(8,128)(2,1)S(1)} %copy-done.12), kind=kOutput, calls=%fused_computation.25 | convolution fusion | flops 1885077504 | bytes 7602176 | tf_op jit(solution)/shard_map/dot_general | solution.py:81
  221.2 4.1 %fusion.12 = bf16[1,1792,1024]{2,1,0:T(8,128)(2,1)} fusion(bf16[512,1792]{1,0:T(8,128)(2,1)S(1)} %bitcast.77, bf16[512,1024]{1,0:T(8,128)(2,1)S(1)} %copy-done.8, bf16[512,1024]{1,0:T(8,128)(2,1)S(1)} %copy-done.10, bf16[512,1024]{1,0:T(8,128)(2,1)S(1)} %copy-done.12), kind=kOutput, calls=%fused_computation.24 | convolution fusion | flops 1887698944 | bytes 8650752 | tf_op jit(solution)/shard_map/dot_general | solution.py:78
  225.4 10.9 %all-to-all-done.3 = bf16[32,16,1792]{2,1,0:T(8,128)(2,1)S(1)} async-done(((bf16[32,16,1792]{2,1,0:T(8,128)(2,1)}), bf16[32,16,1792]{2,1,0:T(8,128)(2,1)S(1)}, u32[]{:S(2)}, u32[]{:S(2)}) %all-to-all-start.3) | async-done | bytes 1835040 | tf_op jit(solution)/shard_map/all_to_all | solution.py:91
  236.2 10.7 %gather_fusion.3 = bf16[2048,1792]{1,0:T(8,128)(2,1)} fusion(bf16[512,1792]{1,0:T(8,128)(2,1)S(1)} %bitcast.71, s32[2048]{0:T(1024)S(1)} %broadcast_clamp_fusion), kind=kCustom, calls=%fused_computation.3 | custom fusion | bytes 14688256 | tf_op jit(solution)/shard_map/gather | solution.py:94
  246.9 7.8 %fusion = bf16[256,1792]{1,0:T(8,128)(2,1)} fusion(bf16[2048,1792]{1,0:T(8,128)(2,1)} %gather_fusion.3, pred[256,8]{1,0:T(8,128)(4,1)S(1)} %copy.20), kind=kLoop, calls=%fused_computation.6 | loop fusion | flops 6881280 | bytes 8259584 | tf_op jit(solution)/shard_map/reduce_sum | solution.py:98
  (36 shorter events, 0.2 us)
Async XLA Ops:
  7.2 35.4 %copy-start = (bf16[256,1792]{1,0:T(8,128)(2,1)S(1)}, bf16[256,1792]{1,0:T(8,128)(2,1)}, u32[]{:S(2)}) copy-start(bf16[256,1792]{1,0:T(8,128)(2,1)} %param.8) | copy-start | bytes 2752516
  7.2 21.2 %copy-start.4 = (bf16[256,8]{0,1:T(8,128)(2,1)S(1)}, bf16[256,8]{0,1:T(8,128)(2,1)}, u32[]{:S(2)}) copy-start(bf16[256,8]{0,1:T(8,128)(2,1)} %param.10) | copy-start | bytes 12292
  32.9 19.6 %all-to-all-start = ((bf16[32,1,16]{2,1,0:T(2,128)(2,1)}), bf16[32,1,16]{2,1,0:T(2,128)(2,1)S(1)}, u32[]{:S(2)}, u32[]{:S(2)}) async-start(bf16[32,1,16]{2,1,0:T(2,128)(2,1)} %all_to_all.20), calls=%async_computation | async-start | bytes 32768 | tf_op jit(solution)/shard_map/all_to_all | solution.py:48
  42.6 3.1 %copy-start.1 = (bf16[256,1792]{1,0:T(8,128)(2,1)S(1)}, bf16[256,1792]{1,0:T(8,128)(2,1)}, u32[]{:S(2)}) copy-start(bf16[256,1792]{1,0:T(8,128)(2,1)} %param.7) | copy-start | bytes 2752516
  85.2 29.3 %all-to-all-start.1 = ((bf16[32,16,1792]{2,1,0:T(8,128)(2,1)}), bf16[32,16,1792]{2,1,0:T(8,128)(2,1)S(1)}, u32[]{:S(2)}, u32[]{:S(2)}) async-start(bf16[32,16,1792]{2,1,0:T(8,128)(2,1)} %get-tuple-element.11), calls=%async_computation.1 | async-start | bytes 3670016 | tf_op jit(solution)/shard_map/all_to_all | solution.py:47
  89.0 104.3 %all-reduce.3.cloned.1.call-start = ((), (), s32[]{:S(2)}) async-start(), calls=%async_computation.4 | async-start | bytes 6291456 | tf_op jit(solution)/shard_map/psum | solution.py:66
  89.3 5.8 %copy-start.2 = (bf16[32,16,1792]{2,1,0:T(8,128)(2,1)S(1)}, bf16[32,16,1792]{2,1,0:T(8,128)(2,1)}, u32[]{:S(2)}) copy-start(bf16[32,16,1792]{2,1,0:T(8,128)(2,1)} %all_to_all.25) | copy-start | bytes 5505028
  89.3 5.8 %copy-start.6 = (bf16[1,1792,1024]{2,1,0:T(8,128)(2,1)S(1)}, bf16[1,1792,1024]{2,1,0:T(8,128)(2,1)}, u32[]{:S(2)}) copy-start(bf16[1,1792,1024]{2,1,0:T(8,128)(2,1)} %param.11) | copy-start | bytes 11010052
  114.5 2.0 copy-start.5
  193.3 6.0 %copy-start.7 = (bf16[1,1792,1024]{2,1,0:T(8,128)(2,1)S(1)}, bf16[1,1792,1024]{2,1,0:T(8,128)(2,1)}, u32[]{:S(2)}) copy-start(bf16[1,1792,1024]{2,1,0:T(8,128)(2,1)} %param.12) | copy-start | bytes 11010052
  193.3 6.0 %copy-start.9 = (bf16[512,1024]{1,0:T(8,128)(2,1)S(1)}, bf16[512,1024]{1,0:T(8,128)(2,1)}, u32[]{:S(2)}) copy-start(bf16[512,1024]{1,0:T(8,128)(2,1)} %get-tuple-element.5) | copy-start | bytes 3145732
  193.3 6.0 %copy-start.11 = (bf16[512,1024]{1,0:T(8,128)(2,1)S(1)}, bf16[512,1024]{1,0:T(8,128)(2,1)}, u32[]{:S(2)}) copy-start(bf16[512,1024]{1,0:T(8,128)(2,1)} %get-tuple-element.6) | copy-start | bytes 3145732
  203.0 33.2 %all-to-all-start.3 = ((bf16[32,16,1792]{2,1,0:T(8,128)(2,1)}), bf16[32,16,1792]{2,1,0:T(8,128)(2,1)S(1)}, u32[]{:S(2)}, u32[]{:S(2)}) async-start(bf16[32,16,1792]{2,1,0:T(8,128)(2,1)} %bitcast.78), calls=%async_computation.3 | async-start | bytes 3670016 | tf_op jit(solution)/shard_map/all_to_all | solution.py:91
  210.8 6.4 %copy-start.3 = (bf16[32,16,1792]{2,1,0:T(8,128)(2,1)S(1)}, bf16[32,16,1792]{2,1,0:T(8,128)(2,1)}, u32[]{:S(2)}) copy-start(bf16[32,16,1792]{2,1,0:T(8,128)(2,1)} %all_to_all.25) | copy-start | bytes 5505028
  210.8 6.4 %copy-start.10 = (bf16[512,1024]{1,0:T(8,128)(2,1)S(1)}, bf16[512,1024]{1,0:T(8,128)(2,1)}, u32[]{:S(2)}) copy-start(bf16[512,1024]{1,0:T(8,128)(2,1)} %get-tuple-element.5) | copy-start | bytes 3145732
  210.8 6.4 %copy-start.12 = (bf16[512,1024]{1,0:T(8,128)(2,1)S(1)}, bf16[512,1024]{1,0:T(8,128)(2,1)}, u32[]{:S(2)}) copy-start(bf16[512,1024]{1,0:T(8,128)(2,1)} %get-tuple-element.6) | copy-start | bytes 3145732
  217.2 4.1 %copy-start.8 = (bf16[512,1024]{1,0:T(8,128)(2,1)S(1)}, bf16[512,1024]{1,0:T(8,128)(2,1)}, u32[]{:S(2)}) copy-start(bf16[512,1024]{1,0:T(8,128)(2,1)} %get-tuple-element.4) | copy-start | bytes 3145732
Sparse Core Ops, SparseCore 0:
  119.8 73.5 all-reduce.2
where the time goes:
time: 262 us
  waiting for transfers between devices  99.2 us (38%)
  matrix products  36.1 us (14%)
  local copies, waits for them, and re-layouts  33.2 us (13%)
  blocking collectives  32.7 us (12%)
  other arithmetic  24.5 us (9%)
  starting transfers between devices  21.4 us (8%)
  between operations  14.3 us (5%)
    psum x1, waiting for transfers between devices, local(): lax.psum(up_part.astype(jnp.bfloat16), 'dp').astype(jnp.float32)  71.9 us
    all_to_all x1, blocking collectives, local(): lax.all_to_all(sent_rows, 'expert', split_axis=0, concat_axis=0, tiled=True)  32.7 us
    all_to_all x1, waiting for transfers between devices, local(): lax.all_to_all(sent_cot, 'expert', split_axis=0, concat_axis=0, tiled=True)  16.4 us
    all_to_all x1, waiting for transfers between devices, local(): lax.all_to_all(contrib, 'expert', split_axis=0, concat_axis=0, tiled=True)  10.9 us
    gather x1, local copies, waits for them, and re-layouts, local(): per_pick = returned[jnp.minimum(target, slot_count - 1)]  10.7 us
    all_to_all x1, starting transfers between devices, local(): lax.all_to_all(sent_coef, 'expert', split_axis=0, concat_axis=0, tiled=True)  9.6 us
    another operation x3, other arithmetic  9.41 us
    scatter x1, local copies, waits for them, and re-layouts, local(): holder = jnp.zeros((slot_count,), jnp.int32).at[target].set(jnp.arange(1,...  8.04 us
  transfers between devices with their start and end apart: 4, of which 3 were waited for; matrix products, arithmetic and copies ran while one was open for 13% of the time, Pallas kernels for 0%

commit v1 on v0

v1 whole, which is shorter than its diff:
```python
import functools

import jax
import jax.numpy as jnp
from jax import lax
from jax.experimental import pallas as pl
from jax.experimental.pallas import tpu as pltpu
from jax.sharding import PartitionSpec as P

MESH = pl.DeviceIdType.MESH
BF16 = jnp.bfloat16
F32 = jnp.float32
N = 4
CAP = 16
CH = 128


def slot_expert(s, y, z, c):
    d, dy, dc = s >> 7, (s >> 5) & 3, (s >> 4) & 1
    dz = (d - dy) & 3
    return (((y + dy) & 3) << 3) + (((z + dz) & 3) << 1) + ((c + dc) & 1)


def dot(a, b):
    return jnp.dot(a, b, preferred_element_type=F32)


def dot_nt(a, b):
    return lax.dot_general(a, b, (((1,), (1,)), ((), ())), preferred_element_type=F32)


def body(
    tok, cot, ids, coef, wg_h, wu_h, wd_h,
    gt, x_o, c_o, hid_o, bg_o, bu_o,
    wg, wu, wd, st, wt, sel, xs, xr, xf, gu, hh, gu_r, hh_r, ag, ct, rz, ry,
    w_sem, ys, yr, zs, zr, loc, rss, rsr, ags, agr, rzs, rzr, rloc, rys, ryr, xo_sem, ho_sem,
):
    tokens_n = tok.shape[0]
    ff = wg.shape[1]
    x = lax.axis_index("dp")
    e = lax.axis_index("expert")
    y, z, c = lax.div(e, 8), lax.rem(lax.div(e, 2), 4), lax.rem(e, 2)

    def at(dx, dy, dz, dc):
        ny, nz, nc = lax.rem(y + dy, 4), lax.rem(z + dz, 4), lax.rem(c + dc, 2)
        return (lax.rem(x + dx, 4), ny * 8 + nz * 2 + nc)

    weights = [
        pltpu.make_async_copy(src, dst, w_sem.at[i])
        for i, (src, dst) in enumerate(((wg_h, wg), (wu_h, wu), (wd_h, wd)))
    ]
    for w in weights:
        w.start()
    barrier = pltpu.get_barrier_semaphore()
    peers = (
        [(0, k, 0, 0) for k in range(1, 4)]
        + [(0, 0, dz, dc) for dz in range(4) for dc in range(2) if dz or dc]
        + [(k, 0, 0, 0) for k in range(1, 4)]
    )
    for p in peers:
        pl.semaphore_signal(barrier, inc=1, device_id=at(*p), device_id_type=MESH)

    experts = lax.broadcasted_iota(jnp.int32, (tokens_n, 32), 1)
    hot, share = jnp.zeros((tokens_n, 32), F32), jnp.zeros((tokens_n, 32), F32)
    idv, cov = ids[...], coef[...].astype(F32)
    for k in range(ids.shape[1]):
        m = idv[:, k : k + 1] == experts
        hot = hot + jnp.where(m, 1.0, 0.0)
        share = share + jnp.where(m, cov[:, k : k + 1], 0.0)
    hot, share = hot.astype(BF16), share.astype(BF16)
    r_io = lax.broadcasted_iota(jnp.int32, (tokens_n, tokens_n), 0)
    c_io = lax.broadcasted_iota(jnp.int32, (tokens_n, tokens_n), 1)
    before = dot(jnp.where(c_io < r_io, 1.0, 0.0).astype(BF16), hot).astype(BF16)
    slots = N * CH
    s_r = lax.broadcasted_iota(jnp.int32, (slots, 32), 0)
    e_r = lax.broadcasted_iota(jnp.int32, (slots, 32), 1)
    to_slot = jnp.where(slot_expert(s_r, y, z, c) == e_r, 1.0, 0.0).astype(BF16)
    row_r = (lax.broadcasted_iota(jnp.int32, (slots, tokens_n), 0) & 15).astype(F32)
    here = (dot_nt(to_slot, hot) > 0.5) & (dot_nt(to_slot, before) == row_r)
    st[...] = jnp.where(here, 1.0, 0.0).astype(BF16)
    wt[...] = jnp.where(here, dot_nt(to_slot, share), 0.0).astype(BF16)

    def dispatch(a, d):
        mat, rows = ((st, tok), (wt, cot))[a]
        xs[a, d] = dot(mat[d * CH : (d + 1) * CH, :], rows[...]).astype(BF16)

    y_out, z_out, z_loc, rs_out, ag_out = {}, {}, {}, {}, {}
    rz_out, rz_loc, ry_out, outs = {}, {}, {}, []

    def remote(src, dst, send, recv, dev):
        cp = pltpu.make_async_remote_copy(
            src_ref=src, dst_ref=dst, send_sem=send, recv_sem=recv, device_id=dev, device_id_type=MESH
        )
        cp.start()
        return cp

    def send_y(a, d):
        for dy in (2, 1, 3):
            r = pl.ds(dy * 32, 32)
            y_out[a, d, dy] = remote(
                xs.at[a, d, r], xr.at[a, d, r], ys.at[a, d, dy - 1], yr.at[a, d, dy - 1], at(0, dy, 0, 0)
            )

    def send_z(a, d):
        for dy in (0, 1, 3, 2):
            buf = xs if dy == 0 else xr
            if dy:
                y_out[a, d, dy].wait_recv()
            dz = (d - dy) % 4
            for dc in range(2):
                r = pl.ds(dy * 32 + dc * 16, 16)
                if dz == 0 and dc == 0:
                    cp = pltpu.make_async_copy(buf.at[a, d, r], xf.at[a, d, r], loc.at[a, d])
                    cp.start()
                    z_loc[a, d] = cp
                else:
                    i = dy * 2 + dc
                    z_out[a, d, i] = remote(
                        buf.at[a, d, r], xf.at[a, d, r], zs.at[a, d, i], zr.at[a, d, i], at(0, 0, dz, dc)
                    )

    def arrive(a, d):
        z_loc[a, d].wait()
        for i in range(8):
            if (a, d, i) in z_out:
                z_out[a, d, i].wait_recv()
        o = pltpu.make_async_copy(xf.at[a, d], (x_o, c_o)[a].at[pl.ds(d * CH, CH)], xo_sem.at[a, d])
        o.start()
        outs.append(o)

    def scatter(t, d):
        buf, got = ((gu, gu_r), (hh, hh_r))[t]
        for k in (2, 1, 3):
            q = lax.rem(x + k, 4)
            rs_out[t, d, k] = remote(
                buf.at[d, pl.ds(pl.multiple_of(q * 32, 32), 32)],
                got.at[d, k - 1],
                rss.at[t, d, k - 1],
                rsr.at[t, d, k - 1],
                at(k, 0, 0, 0),
            )

    def gate_up(d):
        arrive(0, d)
        if d == 0:
            weights[0].wait()
            weights[1].wait()
        rows = xf[0, d]
        gu[d, :, 0:ff] = dot(rows, wg[...]).astype(BF16)
        gu[d, :, ff : 2 * ff] = dot(rows, wu[...]).astype(BF16)
        scatter(0, d)

    def back(d):
        arrive(1, d)
        if d == 0:
            weights[2].wait()
        hh[d] = dot_nt(xf[1, d], wd[...]).astype(BF16)
        scatter(1, d)

    def finish(d):
        mine = pl.ds(pl.multiple_of(x * 32, 32), 32)
        for t in range(2):
            for k in range(1, 4):
                rs_out[t, d, k].wait_recv()
        pre, gh = gu[d, mine, :].astype(F32), hh[d, mine, :].astype(F32)
        for k in range(3):
            pre = pre + gu_r[d, k].astype(F32)
            gh = gh + hh_r[d, k].astype(F32)
        g, u = pre[:, 0:ff], pre[:, ff : 2 * ff]
        sq = jax.nn.sigmoid(g)
        silu = g * sq
        ag[d, mine, 0:ff] = (silu * u).astype(BF16)
        ag[d, mine, ff : 2 * ff] = (gh * u * sq * (1.0 + g * (1.0 - sq))).astype(BF16)
        ag[d, mine, 2 * ff : 3 * ff] = (gh * silu).astype(BF16)
        for k in (2, 1, 3):
            ag_out[d, k] = remote(
                ag.at[d, mine], ag.at[d, mine], ags.at[d, k - 1], agr.at[d, k - 1], at(k, 0, 0, 0)
            )

    def contrib(d):
        for k in range(1, 4):
            ag_out[d, k].wait_recv()
        for i, o_ref in enumerate((hid_o, bg_o, bu_o)):
            o = pltpu.make_async_copy(
                ag.at[d, :, pl.ds(i * ff, ff)], o_ref.at[pl.ds(d * CH, CH)], ho_sem.at[i, d]
            )
            o.start()
            outs.append(o)
        total = dot_nt(ag[d, :, ff : 2 * ff], wg[...]) + dot_nt(ag[d, :, 2 * ff : 3 * ff], wu[...])
        ct[d] = total.astype(BF16)
        for dy in (2, 1, 3, 0):
            dz = (d - dy) % 4
            land = ry if dy == 0 else rz
            for dc in range(2):
                r = pl.ds(dy * 32 + dc * 16, 16)
                if dz == 0 and dc == 0:
                    cp = pltpu.make_async_copy(ct.at[d, r], land.at[d, r], rloc.at[d])
                    cp.start()
                    rz_loc[d] = cp
                else:
                    i = dy * 2 + dc
                    rz_out[d, i] = remote(
                        ct.at[d, r], land.at[d, r], rzs.at[d, i], rzr.at[d, i], at(0, 0, (4 - dz) % 4, dc)
                    )

    def return_y(d):
        for dy in (2, 1, 3, 0):
            for dc in range(2):
                i = dy * 2 + dc
                if (d, i) in rz_out:
                    rz_out[d, i].wait_recv()
                else:
                    rz_loc[d].wait()
            if dy:
                r = pl.ds(dy * 32, 32)
                ry_out[d, dy] = remote(
                    rz.at[d, r], ry.at[d, r], rys.at[d, dy - 1], ryr.at[d, dy - 1], at(0, 4 - dy, 0, 0)
                )

    dispatch(0, 0)
    pl.semaphore_wait(barrier, len(peers))
    send_y(0, 0)
    dispatch(1, 0)
    send_y(1, 0)
    dispatch(0, 1)
    send_y(0, 1)
    for d in range(1, N):
        for a in range(2):
            if (a, d) != (0, 1):
                dispatch(a, d)
    send_z(0, 0)
    send_y(1, 1)
    send_z(1, 0)
    gate_up(0)
    send_z(0, 1)
    send_y(0, 2)
    back(0)
    send_z(1, 1)
    send_y(1, 2)
    gate_up(1)
    send_z(0, 2)
    send_y(0, 3)
    finish(0)
    back(1)
    send_z(1, 2)
    send_y(1, 3)
    gate_up(2)
    send_z(0, 3)
    finish(1)
    contrib(0)
    back(2)
    send_z(1, 3)
    gate_up(3)
    return_y(0)
    finish(2)
    contrib(1)
    back(3)
    return_y(1)
    finish(3)
    contrib(2)
    s_l = lax.broadcasted_iota(jnp.int32, (32, slots), 1)
    e_l = lax.broadcasted_iota(jnp.int32, (32, slots), 0)
    from_slot = jnp.where(slot_expert(s_l, y, z, c) == e_l, 1.0, 0.0).astype(BF16)
    row_l = (lax.broadcasted_iota(jnp.int32, (tokens_n, slots), 1) & 15).astype(F32)
    here_l = (dot(hot, from_slot) > 0.5) & (dot(before, from_slot) == row_l)
    sel[...] = jnp.where(here_l, 1.0, 0.0).astype(BF16)
    return_y(2)
    contrib(3)
    return_y(3)
    total = None
    for d in range(N):
        for dy in range(1, 4):
            ry_out[d, dy].wait_recv()
        part = dot(sel[:, d * CH : (d + 1) * CH], ry[d])
        total = part if total is None else total + part
    gt[...] = total.astype(BF16)
    for table in (y_out, z_out, rs_out, ag_out, rz_out, ry_out):
        for cp in table.values():
            cp.wait_send()
    for o in outs:
        o.wait()


def local(tokens, cotangent, expert_ids, gate_coef, w_gate, w_up, w_down):
    t_n, dq = tokens.shape
    ff = w_gate.shape[2]
    slots = N * CH
    vm = pl.BlockSpec(memory_space=pltpu.VMEM)
    anym = pl.BlockSpec(memory_space=pl.ANY)
    dma = pltpu.SemaphoreType.DMA
    sds = jax.ShapeDtypeStruct
    gt, x_o, c_o, hid, bg, bu = pl.pallas_call(
        body,
        name="exchange",
        out_shape=(
            sds((t_n, dq), BF16),
            sds((slots, dq), BF16),
            sds((slots, dq), BF16),
            sds((slots, ff), BF16),
            sds((slots, ff), BF16),
            sds((slots, ff), BF16),
        ),
        in_specs=[vm, vm, vm, vm, anym, anym, anym],
        out_specs=(vm, anym, anym, anym, anym, anym),
        scratch_shapes=[
            pltpu.VMEM((dq, ff), BF16),
            pltpu.VMEM((dq, ff), BF16),
            pltpu.VMEM((ff, dq), BF16),
            pltpu.VMEM((slots, t_n), BF16),
            pltpu.VMEM((slots, t_n), BF16),
            pltpu.VMEM((t_n, slots), BF16),
            pltpu.VMEM((2, N, CH, dq), BF16),
            pltpu.VMEM((2, N, CH, dq), BF16),
            pltpu.VMEM((2, N, CH, dq), BF16),
            pltpu.VMEM((N, CH, 2 * ff), BF16),
            pltpu.VMEM((N, CH, ff), BF16),
            pltpu.VMEM((N, 3, 32, 2 * ff), BF16),
            pltpu.VMEM((N, 3, 32, ff), BF16),
            pltpu.VMEM((N, CH, 3 * ff), BF16),
            pltpu.VMEM((N, CH, dq), BF16),
            pltpu.VMEM((N, CH, dq), BF16),
            pltpu.VMEM((N, CH, dq), BF16),
            dma((3,)),
            dma((2, N, 3)),
            dma((2, N, 3)),
            dma((2, N, 8)),
            dma((2, N, 8)),
            dma((2, N)),
            dma((2, N, 3)),
            dma((2, N, 3)),
            dma((N, 3)),
            dma((N, 3)),
            dma((N, 8)),
            dma((N, 8)),
            dma((N,)),
            dma((N, 3)),
            dma((N, 3)),
            dma((2, N)),
            dma((3, N)),
        ],
        compiler_params=pltpu.CompilerParams(
            collective_id=0, has_side_effects=True, vmem_limit_bytes=58 * 2**20
        ),
    )(tokens, cotangent, expert_ids, gate_coef, w_gate[0], w_up[0], w_down[0])
    tn = (((0,), (0,)), ((), ()))
    grad_down = lax.dot_general(hid, c_o, tn, preferred_element_type=F32).astype(BF16)
    grad_gate = lax.dot_general(x_o, bg, tn, preferred_element_type=F32).astype(BF16)
    grad_up = lax.dot_general(x_o, bu, tn, preferred_element_type=F32).astype(BF16)
    return (gt, grad_gate[None], grad_up[None], grad_down[None])


def solution(mesh):
    in_specs = (
        P("expert", "dp"),
        P("expert", "dp"),
        P("expert", None),
        P("expert", None),
        P("expert", "dp", None),
        P("expert", "dp", None),
        P("expert", None, "dp"),
    )
    out_specs = (
        P("expert", "dp"),
        P("expert", "dp", None),
        P("expert", "dp", None),
        P("expert", None, "dp"),
    )
    return jax.shard_map(local, mesh=mesh, in_specs=in_specs, out_specs=out_specs, check_vma=False)
```

time: 262 us -> 137 us (0.52)
  Pallas kernels: 0 us -> 118 us
  waiting for transfers between devices: 99.2 us -> 0 us
  blocking collectives: 32.7 us -> 0 us
  local copies, waits for them, and re-layouts: 33.2 us -> 3.85 us
  other arithmetic: 24.5 us -> 0 us
  matrix products: 36.1 us -> 13.8 us
  starting transfers between devices: 21.4 us -> 0 us
  between operations: 14.3 us -> 0.67 us
    pallas_call x0 -> x1, Pallas kernels: none -> 118 us  [local(): pl.pallas_call(body, name='exchange', out_shape=(sds((t_n, dq), BF16), sd...]
    psum x1 -> x0, waiting for transfers between devices: 71.9 us -> none  [local(): lax.psum(up_part.astype(jnp.bfloat16), 'dp').astype(jnp.float32)]
    all_to_all x1 -> x0, blocking collectives: 32.7 us -> none  [local(): lax.all_to_all(sent_rows, 'expert', split_axis=0, concat_axis=0, tiled=True)]
    all_to_all x3 -> x0, waiting for transfers between devices: 27.3 us -> none  [the longest x1 16.4 us: local(): lax.all_to_all(sent_cot, 'expert', split_axis=0, concat_axis=0, tiled=True)]
    dot_general x8 -> x3, matrix products: 36.1 us -> 13.8 us  [the longest x1 5.87 us: local(): lax.dot_general(x_o, bg, tn, preferred_element_type=F32).astype(BF16)]
    all_to_all x3 -> x0, starting transfers between devices: 21.2 us -> none  [the longest x1 9.6 us: local(): lax.all_to_all(sent_coef, 'expert', split_axis=0, concat_axis=0, tiled=True)]
    gather x4 -> x0, local copies, waits for them, and re-layouts: 20.4 us -> none  [the longest x1 10.7 us: local(): per_pick = returned[jnp.minimum(target, slot_count - 1)]]
    another operation x3 -> x0, other arithmetic: 9.41 us -> none
  transfers between devices with their start and end apart: 4 -> 0, of which waited for: 3 -> 0; matrix products, arithmetic and copies ran while one was open for 13% -> 0% of each run, Pallas kernels for 0% -> 0%
where the time goes in v1:
time: 137 us
  Pallas kernels  118 us (86%)
  matrix products  13.8 us (10%)
  local copies, waits for them, and re-layouts  3.85 us (3%)
    pallas_call x1, Pallas kernels, local(): pl.pallas_call(body, name='exchange', out_shape=(sds((t_n, dq), BF16), sd...  118 us
    dot_general x1, matrix products, local(): lax.dot_general(x_o, bg, tn, preferred_element_type=F32).astype(BF16)  5.87 us
    dot_general x1, matrix products, local(): lax.dot_general(hid, c_o, tn, preferred_element_type=F32).astype(BF16)  3.97 us
    dot_general x1, matrix products, local(): lax.dot_general(x_o, bu, tn, preferred_element_type=F32).astype(BF16)  3.95 us
    unnamed x13, local copies, waits for them, and re-layouts  3.85 us

profile of v1, /device:TPU:1, one launch (start us, length us, event | category | flops | bytes accessed | tf_op | source)
XLA Modules:
  0.0 136.8 jit_solution(9327780975073293918)
XLA Ops:
  0.6 1.4 %copy.12.coef = bf16[256,8]{1,0:T(8,128)(2,1)} copy(bf16[256,8]{0,1:T(8,128)(2,1)} %param.10) | data formatting | bytes 8192 | tf_op args[3]
  2.1 1.5 %copy.11.ids = s32[256,8]{1,0:T(8,128)} copy(s32[256,8]{0,1:T(8,128)} %param.9) | data formatting | bytes 16384 | tf_op args[2]
  3.5 118.5 %exchange.1 = (bf16[256,1792]{1,0:T(8,128)(2,1)}, bf16[512,1792]{1,0:T(8,128)(2,1)}, bf16[512,1792]{1,0:T(8,128)(2,1)}, bf16[512,1024]{1,0:T(8,128)(2,1)}, bf16[...) custom-call(bf16[256,1792]{1,0:T(8,128)(2,1)} %tok.1, bf16[256,1792]{1,0:T(8,128)(2,1)} %cot.1, s32[256,8]{1,0:T(8,128)} %copy.11.ids, ...), custom_call_target="tpu_custom_call" | custom-call | tf_op jit(solution)/shard_map/exchange/pallas_call | solution.py:292
  122.0 0.0 copy-start.2
  122.0 0.0 copy-start.4
  122.0 5.9 %fusion = bf16[1,1792,1024]{2,1,0:T(8,128)(2,1)} fusion(bf16[512,1792]{1,0:T(8,128)(2,1)} %get-tuple-element.11, bf16[512,1024]{1,0:T(8,128)(2,1)} %get-tuple-element.12), kind=kOutput, calls=%fused_computation.3 | convolution fusion | flops 1880883200 | bytes 6553600 | tf_op jit(solution)/shard_map/dot_general | solution.py:347
  127.9 0.0 copy-done.2
  127.9 0.0 copy-done.4
  127.9 0.0 copy-start.1
  127.9 0.0 copy-start.3
  127.9 3.9 %fusion.1 = bf16[1,1792,1024]{2,1,0:T(8,128)(2,1)} fusion(bf16[512,1792]{1,0:T(8,128)(2,1)S(1)} %copy-done.2, bf16[512,1024]{1,0:T(8,128)(2,1)S(1)} %copy-done.4), kind=kOutput, calls=%fused_computation.4 | convolution fusion | flops 1880883200 | bytes 6553600 | tf_op jit(solution)/shard_map/dot_general | solution.py:348
  131.9 0.0 copy-done.1
  131.9 0.0 copy-done.3
  131.9 0.0 copy-start
  131.9 4.0 %fusion.2 = bf16[1,1024,1792]{2,1,0:T(8,128)(2,1)} fusion(bf16[512,1024]{1,0:T(8,128)(2,1)S(1)} %copy-done.3, bf16[512,1792]{1,0:T(8,128)(2,1)S(1)} %copy-done.1), kind=kOutput, calls=%fused_computation.5 | convolution fusion | flops 1880883200 | bytes 6553600 | tf_op jit(solution)/shard_map/dot_general | solution.py:346
  135.8 0.0 copy-done
  135.8 0.9 copy.14
Async XLA Ops:
  122.0 5.9 %copy-start.2 = (bf16[512,1792]{1,0:T(8,128)(2,1)S(1)}, bf16[512,1792]{1,0:T(8,128)(2,1)}, u32[]{:S(2)}) copy-start(bf16[512,1792]{1,0:T(8,128)(2,1)} %get-tuple-element.11) | copy-start | bytes 5505028
  122.0 5.9 %copy-start.4 = (bf16[512,1024]{1,0:T(8,128)(2,1)S(1)}, bf16[512,1024]{1,0:T(8,128)(2,1)}, u32[]{:S(2)}) copy-start(bf16[512,1024]{1,0:T(8,128)(2,1)} %get-tuple-element.13) | copy-start | bytes 3145732
  127.9 4.0 %copy-start.1 = (bf16[512,1792]{1,0:T(8,128)(2,1)S(1)}, bf16[512,1792]{1,0:T(8,128)(2,1)}, u32[]{:S(2)}) copy-start(bf16[512,1792]{1,0:T(8,128)(2,1)} %get-tuple-element.15) | copy-start | bytes 5505028
  127.9 4.0 %copy-start.3 = (bf16[512,1024]{1,0:T(8,128)(2,1)S(1)}, bf16[512,1024]{1,0:T(8,128)(2,1)}, u32[]{:S(2)}) copy-start(bf16[512,1024]{1,0:T(8,128)(2,1)} %get-tuple-element.14) | copy-start | bytes 3145732
  131.9 4.0 %copy-start = (bf16[256,1792]{1,0:T(8,128)(2,1)S(1)}, bf16[256,1792]{1,0:T(8,128)(2,1)}, u32[]{:S(2)}) copy-start(bf16[256,1792]{1,0:T(8,128)(2,1)} %get-tuple-element.20) | copy-start | bytes 2752516

commit v2 on v1

v2 whole, which is shorter than its diff:
```python
import functools

import jax
import jax.numpy as jnp
from jax import lax
from jax.experimental import pallas as pl
from jax.experimental.pallas import tpu as pltpu
from jax.sharding import PartitionSpec as P

MESH = pl.DeviceIdType.MESH
BF16 = jnp.bfloat16
F32 = jnp.float32
N = 4
CAP = 16
CH = 128


def slot_expert(s, y, z, c):
    d, dc, dy = s >> 7, (s >> 6) & 1, (s >> 4) & 3
    dz = (d - dy) & 3
    return (((y + dy) & 3) << 3) + (((z + dz) & 3) << 1) + ((c + dc) & 1)


def dot(a, b):
    return jnp.dot(a, b, preferred_element_type=F32)


def dot_nt(a, b):
    return lax.dot_general(a, b, (((1,), (1,)), ((), ())), preferred_element_type=F32)


def body(
    tok_h, cot_h, ids, coef, wg_h, wu_h, wd_h,
    gt, x_o, c_o, hid_o, bg_o, bu_o,
    tok, cot, wg, wu, wd, st, wt, sel, acc, cs, xs, xr, xf, gu, hh, gu_f, hh_f, gu_n, hh_n, ag, hid, ct, rz, rc, rq,
    w_sem, t_sem, cos, cor, ys, yr, zs, zr, loc, fs, fr, ns, nr, as1, ar1, as2, ar2, hs1, hr1, hs2, hr2,
    rzs, rzr, rloc, rys, ryr, rcs, rcr, xo_sem, ho_sem,
):
    tokens_n, dq = tok.shape
    ff = wg.shape[1]
    x = lax.axis_index("dp")
    e = lax.axis_index("expert")
    y, z, c = lax.div(e, 8), lax.rem(lax.div(e, 2), 4), lax.rem(e, 2)
    xp, xm, xo = lax.rem(x + 1, 4), lax.rem(x + 3, 4), lax.rem(x + 2, 4)

    def at(dx, dy, dz, dc):
        ny, nz, nc = lax.rem(y + dy, 4), lax.rem(z + dz, 4), lax.rem(c + dc, 2)
        return (lax.rem(x + dx, 4), ny * 8 + nz * 2 + nc)

    barrier = pltpu.get_barrier_semaphore()
    peers = (
        [(0, 0, 0, 1)]
        + [(0, k, 0, 0) for k in range(1, 4)]
        + [(0, 0, k, 0) for k in range(1, 4)]
        + [(1, 0, 0, 0), (3, 0, 0, 0)]
    )
    for p in peers:
        pl.semaphore_signal(barrier, inc=1, device_id=at(*p), device_id_type=MESH)

    inputs = [
        pltpu.make_async_copy(src, dst, t_sem.at[i])
        for i, (src, dst) in enumerate(((tok_h, tok), (cot_h, cot)))
    ]
    for i in inputs:
        i.start()
    weights = [
        pltpu.make_async_copy(src, dst, w_sem.at[i])
        for i, (src, dst) in enumerate(((wg_h, wg), (wu_h, wu), (wd_h, wd)))
    ]
    for w in weights:
        w.start()

    experts = lax.broadcasted_iota(jnp.int32, (32, tokens_n), 0)
    hot, share = jnp.zeros((32, tokens_n), F32), jnp.zeros((32, tokens_n), F32)
    idv, cov = ids[...], coef[...].astype(F32)
    for k in range(ids.shape[0]):
        m = idv[k : k + 1, :] == experts
        hot = hot + jnp.where(m, 1.0, 0.0)
        share = share + jnp.where(m, cov[k : k + 1, :], 0.0)
    hot_b, share = hot.astype(BF16), share.astype(BF16)
    r_io = lax.broadcasted_iota(jnp.int32, (tokens_n, tokens_n), 0)
    c_io = lax.broadcasted_iota(jnp.int32, (tokens_n, tokens_n), 1)
    before = dot(hot_b, jnp.where(r_io < c_io, 1.0, 0.0).astype(BF16))
    before_b = before.astype(BF16)
    slots = N * CH
    s_r = lax.broadcasted_iota(jnp.int32, (slots, 32), 0)
    e_r = lax.broadcasted_iota(jnp.int32, (slots, 32), 1)
    to_slot = jnp.where(slot_expert(s_r, y, z, c) == e_r, 1.0, 0.0).astype(BF16)
    row_r = (lax.broadcasted_iota(jnp.int32, (slots, tokens_n), 0) & 15).astype(F32)
    here = (dot(to_slot, hot_b) > 0.5) & (dot(to_slot, before_b) == row_r)
    st[...] = jnp.where(here, 1.0, 0.0).astype(BF16)
    wt[...] = jnp.where(here, dot(to_slot, share), 0.0).astype(BF16)

    core_out, y_out, z_out, z_loc, far, near = {}, {}, {}, {}, {}, {}
    ag1, ag2, hid1, hid2 = {}, {}, {}, {}
    halves = (pl.ds(0, 1024), pl.ds(1024, dq - 1024))
    rz_out, rz_loc, ry_out, rc_out, outs = {}, {}, {}, {}, []

    def remote(table, key, src, dst, send, recv, dev):
        cp = pltpu.make_async_remote_copy(
            src_ref=src, dst_ref=dst, send_sem=send, recv_sem=recv, device_id=dev, device_id_type=MESH
        )
        cp.start()
        table[key] = cp

    def dispatch(a, d):
        mat, rows = ((st, tok), (wt, cot))[a]
        made = dot(mat[d * CH : (d + 1) * CH, :], rows[...]).astype(BF16).reshape(2, 4, CAP, dq)
        xs[a, d, :, 0] = made[0]
        cs[a, d] = made[1]

    def send_core(a, d):
        remote(core_out, (a, d), cs.at[a, d], xs.at[a, d, :, 1], cos.at[a, d], cor.at[a, d], at(0, 0, 0, 1))

    def send_y(a, d):
        core_out[a, d].wait_recv()
        for dy in (2, 1, 3):
            land = xf if dy == d else xr
            remote(
                y_out, (a, d, dy), xs.at[a, d, dy], land.at[a, d, dy],
                ys.at[a, d, dy - 1], yr.at[a, d, dy - 1], at(0, dy, 0, 0),
            )

    def send_z(a, d):
        for dy in (0, 1, 3, 2):
            if dy == d:
                continue
            if dy:
                y_out[a, d, dy].wait_recv()
            remote(
                z_out, (a, d, dy), (xr if dy else xs).at[a, d, dy], xf.at[a, d, dy],
                zs.at[a, d, dy], zr.at[a, d, dy], at(0, 0, (d - dy) % 4, 0),
            )
        if d == 0:
            z_loc[a] = pltpu.make_async_copy(xs.at[a, 0, 0], xf.at[a, 0, 0], loc.at[a])
            z_loc[a].start()

    def arrive(a, d):
        if d == 0:
            z_loc[a].wait()
        else:
            y_out[a, d, d].wait_recv()
        for dy in range(4):
            if dy != d:
                z_out[a, d, dy].wait_recv()
        o = pltpu.make_async_copy(xf.at[a, d], (x_o, c_o)[a].at[d], xo_sem.at[a, d])
        o.start()
        outs.append(o)

    def scatter(t, d):
        buf, f_r, n_r = ((gu, gu_f, gu_n), (hh, hh_f, hh_n))[t]
        for i, dx in ((0, 1), (1, 3)):
            remote(far, (t, d, i), buf.at[d, xo, i], f_r.at[d, i], fs.at[t, d, i], fr.at[t, d, i], at(dx, 0, 0, 0))
        for i, (dx, q) in enumerate(((1, xp), (3, xm))):
            remote(
                near, (t, d, i), buf.at[d, q, 1 - i], n_r.at[d, i, 1 - i],
                ns.at[t, d, i], nr.at[t, d, i], at(dx, 0, 0, 0),
            )

    def scatter_on(t, d):
        buf, f_r, n_r = ((gu, gu_f, gu_n), (hh, hh_f, hh_n))[t]
        for i, (dx, q) in enumerate(((1, xp), (3, xm))):
            far[t, d, i].wait_recv()
            both = buf[d, q, i].astype(F32) + f_r[d, i].astype(F32)
            buf[d, q, i] = both.astype(BF16)
            remote(
                near, (t, d, 2 + i), buf.at[d, q, i], n_r.at[d, i, i],
                ns.at[t, d, 2 + i], nr.at[t, d, 2 + i], at(dx, 0, 0, 0),
            )

    def gate_up(d):
        arrive(0, d)
        if d == 0:
            weights[0].wait()
            weights[1].wait()
        rows = xf[0, d].reshape(CH, dq)
        gu[d, :, :, :, 0:ff] = dot(rows, wg[...]).astype(BF16).reshape(4, 2, CAP, ff)
        gu[d, :, :, :, ff : 2 * ff] = dot(rows, wu[...]).astype(BF16).reshape(4, 2, CAP, ff)
        scatter(0, d)

    def back(d):
        arrive(1, d)
        if d == 0:
            weights[2].wait()
        hh[d] = dot_nt(xf[1, d].reshape(CH, dq), wd[...]).astype(BF16).reshape(4, 2, CAP, ff)
        scatter(1, d)

    def finish(d):
        for t in range(2):
            for i in range(4):
                near[t, d, i].wait_recv()
        pre, gh = gu[d, x].astype(F32), hh[d, x].astype(F32)
        for i in range(2):
            pre = pre + gu_n[d, i].astype(F32)
            gh = gh + hh_n[d, i].astype(F32)
        g, u = pre[:, :, 0:ff], pre[:, :, ff : 2 * ff]
        sq = jax.nn.sigmoid(g)
        silu = g * sq
        hid[d, x] = (silu * u).astype(BF16)
        ag[d, x, :, :, 0:ff] = (gh * u * sq * (1.0 + g * (1.0 - sq))).astype(BF16)
        ag[d, x, :, :, ff : 2 * ff] = (gh * silu).astype(BF16)
        for i, dx in ((0, 1), (1, 3)):
            remote(ag1, (d, i), ag.at[d, x], ag.at[d, x], as1.at[d, i], ar1.at[d, i], at(dx, 0, 0, 0))

    def gather_on(d):
        for i, (dx, q) in enumerate(((1, xm), (3, xp))):
            ag1[d, i].wait_recv()
            remote(ag2, (d, i), ag.at[d, q, i], ag.at[d, q, i], as2.at[d, i], ar2.at[d, i], at(dx, 0, 0, 0))

    def hidden(d):
        for i, dx in ((0, 1), (1, 3)):
            remote(hid1, (d, i), hid.at[d, x], hid.at[d, x], hs1.at[d, i], hr1.at[d, i], at(dx, 0, 0, 0))

    def hidden_on(d):
        for i, (dx, q) in enumerate(((1, xm), (3, xp))):
            hid1[d, i].wait_recv()
            remote(hid2, (d, i), hid.at[d, q, i], hid.at[d, q, i], hs2.at[d, i], hr2.at[d, i], at(dx, 0, 0, 0))

    def keep(src, dst, sem):
        o = pltpu.make_async_copy(src, dst, sem)
        o.start()
        outs.append(o)

    def contrib(d, h):
        if h == 0:
            for i in range(2):
                ag2[d, i].wait_recv()
            for i, o_ref in enumerate((bg_o, bu_o)):
                keep(ag.at[d, :, :, :, pl.ds(i * ff, ff)], o_ref.at[d], ho_sem.at[i, d])
        w = halves[h]
        back_gate = ag[d, :, :, :, 0:ff].reshape(CH, ff)
        back_up = ag[d, :, :, :, ff : 2 * ff].reshape(CH, ff)
        total = dot_nt(back_gate, wg[w, :]) + dot_nt(back_up, wu[w, :])
        ct[d, :, :, :, w] = total.astype(BF16).reshape(4, 2, CAP, w.size)
        for dy in (2, 1, 3, 0):
            dz = (d - dy) % 4
            if dz:
                remote(
                    rz_out, (d, dy, h), ct.at[d, dy, :, :, w], (rz if dy else rc).at[d, dy, :, :, w],
                    rzs.at[d, dy, h], rzr.at[d, dy, h], at(0, 0, 4 - dz, 0),
                )
            elif dy == 0:
                rz_loc[h] = pltpu.make_async_copy(ct.at[d, 0, :, :, w], rc.at[d, 0, :, :, w], rloc.at[h])
                rz_loc[h].start()
            else:
                back_y(ct, d, dy, h)

    def back_y(src, d, dy, h):
        w = halves[h]
        remote(
            ry_out, (d, dy, h), src.at[d, dy, :, :, w], rc.at[d, dy, :, :, w],
            rys.at[d, dy - 1, h], ryr.at[d, dy - 1, h], at(0, 4 - dy, 0, 0),
        )

    def return_y(d, h):
        for dy in (2, 1, 3):
            if dy != d:
                rz_out[d, dy, h].wait_recv()
                back_y(rz, d, dy, h)

    def return_core(d, h):
        if d == 0:
            rz_loc[h].wait()
        else:
            rz_out[d, 0, h].wait_recv()
        for dy in (1, 3, 2):
            ry_out[d, dy, h].wait_recv()
        w = halves[h]
        remote(
            rc_out, (d, h), rc.at[d, :, 1, :, w], rq.at[d, :, :, w], rcs.at[d, h], rcr.at[d, h], at(0, 0, 0, 1)
        )

    def combine(d):
        for h in range(2):
            rc_out[d, h].wait_recv()
        part = dot(sel[:, d * CH : d * CH + 64], rc[d, :, 0].reshape(64, dq))
        part = part + dot(sel[:, d * CH + 64 : (d + 1) * CH], rq[d].reshape(64, dq))
        if d == 0:
            acc[...] = part
        elif d < N - 1:
            acc[...] += part
        else:
            gt[...] = (acc[...] + part).astype(BF16)

    inputs[0].wait()
    dispatch(0, 0)
    pl.semaphore_wait(barrier, len(peers))
    send_core(0, 0)
    inputs[1].wait()
    dispatch(1, 0)
    send_core(1, 0)
    send_y(0, 0)
    dispatch(0, 1)
    send_core(0, 1)
    send_y(1, 0)
    dispatch(1, 1)
    send_core(1, 1)
    send_y(0, 1)
    send_z(0, 0)
    dispatch(0, 2)
    send_core(0, 2)
    send_y(1, 1)
    dispatch(1, 2)
    send_core(1, 2)
    dispatch(0, 3)
    send_core(0, 3)
    dispatch(1, 3)
    send_core(1, 3)
    sel[...] = st[...].astype(F32).T.astype(BF16)
    send_z(1, 0)
    send_y(0, 2)
    gate_up(0)
    send_z(0, 1)
    send_y(1, 2)
    back(0)
    scatter_on(0, 0)
    send_z(1, 1)
    send_y(0, 3)
    scatter_on(1, 0)
    gate_up(1)
    finish(0)
    send_z(0, 2)
    send_y(1, 3)
    back(1)
    scatter_on(0, 1)
    send_z(1, 2)
    gather_on(0)
    scatter_on(1, 1)
    gate_up(2)
    finish(1)
    send_z(0, 3)
    contrib(0, 0)
    back(2)
    contrib(0, 1)
    scatter_on(0, 2)
    send_z(1, 3)
    gather_on(1)
    hidden(0)
    scatter_on(1, 2)
    gate_up(3)
    return_y(0, 0)
    return_y(0, 1)
    back(3)
    finish(2)
    scatter_on(0, 3)
    contrib(1, 0)
    scatter_on(1, 3)
    contrib(1, 1)
    gather_on(2)
    hidden(1)
    hidden_on(0)
    finish(3)
    return_y(1, 0)
    return_y(1, 1)
    contrib(2, 0)
    gather_on(3)
    contrib(2, 1)
    hidden(2)
    hidden(3)
    return_y(2, 0)
    contrib(3, 0)
    return_y(2, 1)
    contrib(3, 1)
    hidden_on(1)
    return_core(0, 0)
    return_core(0, 1)
    return_core(1, 0)
    return_core(1, 1)
    combine(0)
    return_y(3, 0)
    return_y(3, 1)
    hidden_on(2)
    hidden_on(3)
    return_core(2, 0)
    return_core(2, 1)
    combine(1)
    return_core(3, 0)
    return_core(3, 1)
    combine(2)
    combine(3)
    for d in range(N):
        for i in range(2):
            hid2[d, i].wait_recv()
        keep(hid.at[d], hid_o.at[d], ho_sem.at[2, d])
    for table in (core_out, y_out, z_out, far, near, ag1, ag2, hid1, hid2, rz_out, ry_out, rc_out):
        for cp in table.values():
            cp.wait_send()
    for o in outs:
        o.wait()


def grads_body(x_ref, c_ref, hid, bg, bu, gg, gup, gd, hid_t):
    @pl.when(pl.program_id(0) == 0)
    def _():
        hid_t[...] = hid[...].T

    x_t = x_ref[...].T
    gg[...] = dot(x_t, bg[...]).astype(BF16)
    gup[...] = dot(x_t, bu[...]).astype(BF16)
    gd[...] = dot(hid_t[...], c_ref[...]).astype(BF16)


def grads(x_rows, c_rows, hid, bg, bu):
    slots, dq = x_rows.shape
    ff = hid.shape[1]
    tile = 256
    sds = jax.ShapeDtypeStruct
    whole = pl.BlockSpec((slots, ff), lambda i: (0, 0))
    cols = pl.BlockSpec((slots, tile), lambda i: (0, i))
    rows = pl.BlockSpec((tile, ff), lambda i: (i, 0))
    return pl.pallas_call(
        grads_body,
        name="grads",
        grid=(dq // tile,),
        out_shape=(sds((dq, ff), BF16), sds((dq, ff), BF16), sds((ff, dq), BF16)),
        in_specs=[cols, cols, whole, whole, whole],
        out_specs=(rows, rows, pl.BlockSpec((ff, tile), lambda i: (0, i))),
        scratch_shapes=[pltpu.VMEM((ff, slots), BF16)],
        compiler_params=pltpu.CompilerParams(vmem_limit_bytes=60 * 2**20),
    )(x_rows, c_rows, hid, bg, bu)


def local(tokens, cotangent, expert_ids, gate_coef, w_gate, w_up, w_down):
    t_n, dq = tokens.shape
    ff = w_gate.shape[2]
    slots = N * CH
    vm = pl.BlockSpec(memory_space=pltpu.VMEM)
    anym = pl.BlockSpec(memory_space=pl.ANY)
    dma = pltpu.SemaphoreType.DMA
    sds = jax.ShapeDtypeStruct

    def rows(*shape):
        return pltpu.VMEM(shape, BF16)

    block = (4, 2, CAP)
    gt, x_o, c_o, hid, bg, bu = pl.pallas_call(
        body,
        name="exchange",
        out_shape=(
            sds((t_n, dq), BF16),
            sds((N, *block, dq), BF16),
            sds((N, *block, dq), BF16),
            sds((N, *block, ff), BF16),
            sds((N, *block, ff), BF16),
            sds((N, *block, ff), BF16),
        ),
        in_specs=[anym, anym, vm, vm, anym, anym, anym],
        out_specs=(vm, anym, anym, anym, anym, anym),
        scratch_shapes=[
            rows(t_n, dq),
            rows(t_n, dq),
            rows(dq, ff),
            rows(dq, ff),
            rows(ff, dq),
            rows(slots, t_n),
            rows(slots, t_n),
            rows(t_n, slots),
            pltpu.VMEM((t_n, dq), F32),
            rows(2, N, 4, CAP, dq),
            rows(2, N, *block, dq),
            rows(2, N, *block, dq),
            rows(2, N, *block, dq),
            rows(N, *block, 2 * ff),
            rows(N, *block, ff),
            rows(N, 2, CAP, 2 * ff),
            rows(N, 2, CAP, ff),
            rows(N, 2, 2, CAP, 2 * ff),
            rows(N, 2, 2, CAP, ff),
            rows(N, *block, 2 * ff),
            rows(N, *block, ff),
            rows(N, *block, dq),
            rows(N, *block, dq),
            rows(N, *block, dq),
            rows(N, 4, CAP, dq),
            dma((3,)),
            dma((2,)),
            dma((2, N)),
            dma((2, N)),
            dma((2, N, 3)),
            dma((2, N, 3)),
            dma((2, N, 4)),
            dma((2, N, 4)),
            dma((2,)),
            dma((2, N, 2)),
            dma((2, N, 2)),
            dma((2, N, 4)),
            dma((2, N, 4)),
            dma((N, 2)),
            dma((N, 2)),
            dma((N, 2)),
            dma((N, 2)),
            dma((N, 2)),
            dma((N, 2)),
            dma((N, 2)),
            dma((N, 2)),
            dma((N, 4, 2)),
            dma((N, 4, 2)),
            dma((2,)),
            dma((N, 3, 2)),
            dma((N, 3, 2)),
            dma((N, 2)),
            dma((N, 2)),
            dma((2, N)),
            dma((3, N)),
        ],
        compiler_params=pltpu.CompilerParams(
            collective_id=0, has_side_effects=True, vmem_limit_bytes=58 * 2**20
        ),
    )(tokens, cotangent, expert_ids.T, gate_coef.T, w_gate[0], w_up[0], w_down[0])
    grad_gate, grad_up, grad_down = grads(
        x_o.reshape(slots, dq),
        c_o.reshape(slots, dq),
        hid.reshape(slots, ff),
        bg.reshape(slots, ff),
        bu.reshape(slots, ff),
    )
    return (gt, grad_gate[None], grad_up[None], grad_down[None])


def solution(mesh):
    in_specs = (
        P("expert", "dp"),
        P("expert", "dp"),
        P("expert", None),
        P("expert", None),
        P("expert", "dp", None),
        P("expert", "dp", None),
        P("expert", None, "dp"),
    )
    out_specs = (
        P("expert", "dp"),
        P("expert", "dp", None),
        P("expert", "dp", None),
        P("expert", None, "dp"),
    )
    return jax.shard_map(local, mesh=mesh, in_specs=in_specs, out_specs=out_specs, check_vma=False)
```

time: 137 us -> 119 us (0.87)
  matrix products: 13.8 us -> 0 us
  local copies, waits for them, and re-layouts: 3.85 us -> 0.93 us
    dot_general x3 -> x0, matrix products: 13.8 us -> none  [the longest x1 5.87 us: local(): lax.dot_general(x_o, bg, tn, preferred_element_type=F32).astype(BF16)]
    pallas_call x1, Pallas kernels: 118 us -> 106 us  [local(): pl.pallas_call(body, name='exchange', out_shape=(sds((t_n, dq), BF16), sd...]
    pallas_call x0 -> x1, Pallas kernels: none -> 11 us  [grads(): pl.pallas_call(grads_body, name='grads', grid=(dq // tile,), out_shape=(s...]
    unnamed x13 -> x3, local copies, waits for them, and re-layouts: 3.85 us -> 0.93 us
where the time goes in v2:
time: 119 us
  Pallas kernels  117 us (98%)
    pallas_call x1, Pallas kernels, local(): pl.pallas_call(body, name='exchange', out_shape=(sds((t_n, dq), BF16), sd...  106 us
    pallas_call x1, Pallas kernels, grads(): pl.pallas_call(grads_body, name='grads', grid=(dq // tile,), out_shape=(s...  11 us

profile of v2, /device:TPU:1, one launch (start us, length us, event | category | flops | bytes accessed | tf_op | source)
XLA Modules:
  0.0 118.9 jit_solution(10412396630332928010)
XLA Ops:
  0.6 106.4 %exchange.1 = (bf16[256,1792]{1,0:T(8,128)(2,1)}, bf16[4,4,2,16,1792]{4,3,2,1,0:T(8,128)(2,1)}, bf16[4,4,2,16,1792]{4,3,2,1,0:T(8,128)(2,1)}, bf16[4,4,2,16,1024...) custom-call(bf16[256,1792]{1,0:T(8,128)(2,1)} %tok_h.1, ...), custom_call_target="tpu_custom_call" | custom-call | tf_op jit(solution)/shard_map/exchange/pallas_call | solution.py:436
  107.0 0.0 copy-start
  107.0 11.0 %grads.1 = (bf16[1792,1024]{1,0:T(8,128)(2,1)}, bf16[1792,1024]{1,0:T(8,128)(2,1)}, bf16[1024,1792]{1,0:T(8,128)(2,1)}) custom-call(bf16[512,1792]{1,0:T(8,128)(2,1)} %bitcast.16, bf16[512,1792]{1,0:T(8,128)(2,1)} %bitcast.17, bf16[512,1024]{1,0:T(8,128)(2,1)} %bitcast.18, bf16[512,1024]{1,0:T(8,128)(2,1)} %bitcast.19, bf16[512,1024]{1,0:T(8,128)(2,1)} %bitcast.20), custom_call_target="tpu_custom_call" | custom-call | tf_op jit(solution)/shard_map/grads/pallas_call | solution.py:411
  118.0 0.0 copy-done
  118.0 0.9 copy.12
Async XLA Ops:
  107.0 11.0 %copy-start = (bf16[256,1792]{1,0:T(8,128)(2,1)S(1)}, bf16[256,1792]{1,0:T(8,128)(2,1)}, u32[]{:S(2)}) copy-start(bf16[256,1792]{1,0:T(8,128)(2,1)} %get-tuple-element.26) | copy-start | bytes 2752516

commit v3 on v2

--- a/solution.py
+++ b/solution.py
@@ -94,6 +94,7 @@
     core_out, y_out, z_out, z_loc, far, near = {}, {}, {}, {}, {}, {}
     ag1, ag2, hid1, hid2 = {}, {}, {}, {}
     halves = (pl.ds(0, 1024), pl.ds(1024, dq - 1024))
+    route = (pl.ds(0, dq // 2), pl.ds(dq // 2, dq // 2))
     rz_out, rz_loc, ry_out, rc_out, outs = {}, {}, {}, {}, []
 
     def remote(table, key, src, dst, send, recv, dev):
@@ -112,37 +113,47 @@
     def send_core(a, d):
         remote(core_out, (a, d), cs.at[a, d], xs.at[a, d, :, 1], cos.at[a, d], cor.at[a, d], at(0, 0, 0, 1))
 
+    def hop(axis, k):
+        return at(0, k, 0, 0) if axis == 0 else at(0, 0, k, 0)
+
+    def paths(d):
+        for dy in (2, 1, 3, 0):
+            off = (dy, (d - dy) % 4)
+            for r in range(2):
+                yield dy, r, off[r], off[1 - r]
+
     def send_y(a, d):
         core_out[a, d].wait_recv()
-        for dy in (2, 1, 3):
-            land = xf if dy == d else xr
-            remote(
-                y_out, (a, d, dy), xs.at[a, d, dy], land.at[a, d, dy],
-                ys.at[a, d, dy - 1], yr.at[a, d, dy - 1], at(0, dy, 0, 0),
-            )
+        for dy, r, f, g in paths(d):
+            if f:
+                w = route[r]
+                remote(
+                    y_out, (a, d, dy, r), xs.at[a, d, dy, :, :, w], (xr if g else xf).at[a, d, dy, :, :, w],
+                    ys.at[a, d, dy, r], yr.at[a, d, dy, r], hop(r, f),
+                )
 
     def send_z(a, d):
-        for dy in (0, 1, 3, 2):
-            if dy == d:
-                continue
-            if dy:
-                y_out[a, d, dy].wait_recv()
-            remote(
-                z_out, (a, d, dy), (xr if dy else xs).at[a, d, dy], xf.at[a, d, dy],
-                zs.at[a, d, dy], zr.at[a, d, dy], at(0, 0, (d - dy) % 4, 0),
-            )
         if d == 0:
             z_loc[a] = pltpu.make_async_copy(xs.at[a, 0, 0], xf.at[a, 0, 0], loc.at[a])
             z_loc[a].start()
+        for dy, r, f, g in sorted(paths(d), key=lambda p: p[2] % 4 == 2):
+            if g:
+                if f:
+                    y_out[a, d, dy, r].wait_recv()
+                w = route[r]
+                remote(
+                    z_out, (a, d, dy, r), (xr if f else xs).at[a, d, dy, :, :, w], xf.at[a, d, dy, :, :, w],
+                    zs.at[a, d, dy, r], zr.at[a, d, dy, r], hop(1 - r, g),
+                )
 
     def arrive(a, d):
         if d == 0:
             z_loc[a].wait()
-        else:
-            y_out[a, d, d].wait_recv()
-        for dy in range(4):
-            if dy != d:
-                z_out[a, d, dy].wait_recv()
+        for dy, r, f, g in paths(d):
+            if g:
+                z_out[a, d, dy, r].wait_recv()
+            elif f:
+                y_out[a, d, dy, r].wait_recv()
         o = pltpu.make_async_copy(xf.at[a, d], (x_o, c_o)[a].at[d], xo_sem.at[a, d])
         o.start()
         outs.append(o)
@@ -232,39 +243,44 @@
         back_up = ag[d, :, :, :, ff : 2 * ff].reshape(CH, ff)
         total = dot_nt(back_gate, wg[w, :]) + dot_nt(back_up, wu[w, :])
         ct[d, :, :, :, w] = total.astype(BF16).reshape(4, 2, CAP, w.size)
-        for dy in (2, 1, 3, 0):
-            dz = (d - dy) % 4
-            if dz:
+        for dy, f, g in ways_back(d, h):
+            if f:
                 remote(
-                    rz_out, (d, dy, h), ct.at[d, dy, :, :, w], (rz if dy else rc).at[d, dy, :, :, w],
-                    rzs.at[d, dy, h], rzr.at[d, dy, h], at(0, 0, 4 - dz, 0),
+                    rz_out, (d, dy, h), ct.at[d, dy, :, :, w], (rz if g else rc).at[d, dy, :, :, w],
+                    rzs.at[d, dy, h], rzr.at[d, dy, h], hop(1 - h, 4 - f),
                 )
-            elif dy == 0:
+            elif g:
+                second_back(ct, d, dy, h, g)
+            else:
                 rz_loc[h] = pltpu.make_async_copy(ct.at[d, 0, :, :, w], rc.at[d, 0, :, :, w], rloc.at[h])
                 rz_loc[h].start()
-            else:
-                back_y(ct, d, dy, h)
-
-    def back_y(src, d, dy, h):
+
+    def ways_back(d, h):
+        for dy in (2, 1, 3, 0):
+            off = ((d - dy) % 4, dy)
+            yield dy, off[h], off[1 - h]
+
+    def second_back(src, d, dy, h, g):
         w = halves[h]
         remote(
             ry_out, (d, dy, h), src.at[d, dy, :, :, w], rc.at[d, dy, :, :, w],
-            rys.at[d, dy - 1, h], ryr.at[d, dy - 1, h], at(0, 4 - dy, 0, 0),
+            rys.at[d, dy, h], ryr.at[d, dy, h], hop(h, 4 - g),
         )
 
     def return_y(d, h):
-        for dy in (2, 1, 3):
-            if dy != d:
+        for dy, f, g in sorted(ways_back(d, h), key=lambda p: p[1] == 2):
+            if f and g:
                 rz_out[d, dy, h].wait_recv()
-                back_y(rz, d, dy, h)
+                second_back(rz, d, dy, h, g)
 
     def return_core(d, h):
-        if d == 0:
-            rz_loc[h].wait()
-        else:
-            rz_out[d, 0, h].wait_recv()
-        for dy in (1, 3, 2):
-            ry_out[d, dy, h].wait_recv()
+        for dy, f, g in ways_back(d, h):
+            if g:
+                ry_out[d, dy, h].wait_recv()
+            elif f:
+                rz_out[d, dy, h].wait_recv()
+            else:
+                rz_loc[h].wait()
         w = halves[h]
         remote(
             rc_out, (d, h), rc.at[d, :, 1, :, w], rq.at[d, :, :, w], rcs.at[d, h], rcr.at[d, h], at(0, 0, 0, 1)
@@ -476,10 +492,10 @@
             dma((2,)),
             dma((2, N)),
             dma((2, N)),
-            dma((2, N, 3)),
-            dma((2, N, 3)),
-            dma((2, N, 4)),
-            dma((2, N, 4)),
+            dma((2, N, 4, 2)),
+            dma((2, N, 4, 2)),
+            dma((2, N, 4, 2)),
+            dma((2, N, 4, 2)),
             dma((2,)),
             dma((2, N, 2)),
             dma((2, N, 2)),
@@ -496,8 +512,8 @@
             dma((N, 4, 2)),
             dma((N, 4, 2)),
             dma((2,)),
-            dma((N, 3, 2)),
-            dma((N, 3, 2)),
+            dma((N, 4, 2)),
+            dma((N, 4, 2)),
             dma((N, 2)),
             dma((N, 2)),
             dma((2, N)),

time: 119 us -> 114 us (0.958)
  Pallas kernels: 117 us -> 112 us
    pallas_call x1, Pallas kernels: 106 us -> 101 us  [local(): pl.pallas_call(body, name='exchange', out_shape=(sds((t_n, dq), BF16), sd...]
where the time goes in v3:
time: 114 us
  Pallas kernels  112 us (98%)
    pallas_call x1, Pallas kernels, local(): pl.pallas_call(body, name='exchange', out_shape=(sds((t_n, dq), BF16), sd...  101 us
    pallas_call x1, Pallas kernels, grads(): pl.pallas_call(grads_body, name='grads', grid=(dq // tile,), out_shape=(s...  11 us

profile of v3, /device:TPU:1, one launch (start us, length us, event | category | flops | bytes accessed | tf_op | source)
XLA Modules:
  0.0 113.8 jit_solution(5052116301612162273)
XLA Ops:
  0.6 101.2 %exchange.1 = (bf16[256,1792]{1,0:T(8,128)(2,1)}, bf16[4,4,2,16,1792]{4,3,2,1,0:T(8,128)(2,1)}, bf16[4,4,2,16,1792]{4,3,2,1,0:T(8,128)(2,1)}, bf16[4,4,2,16,1024...) custom-call(bf16[256,1792]{1,0:T(8,128)(2,1)} %tok_h.1, ...), custom_call_target="tpu_custom_call" | custom-call | tf_op jit(solution)/shard_map/exchange/pallas_call | solution.py:452
  101.9 0.0 copy-start
  101.9 11.0 %grads.1 = (bf16[1792,1024]{1,0:T(8,128)(2,1)}, bf16[1792,1024]{1,0:T(8,128)(2,1)}, bf16[1024,1792]{1,0:T(8,128)(2,1)}) custom-call(bf16[512,1792]{1,0:T(8,128)(2,1)} %bitcast.16, bf16[512,1792]{1,0:T(8,128)(2,1)} %bitcast.17, bf16[512,1024]{1,0:T(8,128)(2,1)} %bitcast.18, bf16[512,1024]{1,0:T(8,128)(2,1)} %bitcast.19, bf16[512,1024]{1,0:T(8,128)(2,1)} %bitcast.20), custom_call_target="tpu_custom_call" | custom-call | tf_op jit(solution)/shard_map/grads/pallas_call | solution.py:427
  112.9 0.0 copy-done
  112.9 0.9 copy.12
Async XLA Ops:
  101.9 11.0 %copy-start = (bf16[256,1792]{1,0:T(8,128)(2,1)S(1)}, bf16[256,1792]{1,0:T(8,128)(2,1)}, u32[]{:S(2)}) copy-start(bf16[256,1792]{1,0:T(8,128)(2,1)} %get-tuple-element.26) | copy-start | bytes 2752516

commit v4 on v3

--- a/solution.py
+++ b/solution.py
@@ -351,7 +351,6 @@
     scatter_on(0, 2)
     send_z(1, 3)
     gather_on(1)
-    hidden(0)
     scatter_on(1, 2)
     gate_up(3)
     return_y(0, 0)
@@ -361,23 +360,22 @@
     scatter_on(0, 3)
     contrib(1, 0)
     scatter_on(1, 3)
+    gather_on(2)
     contrib(1, 1)
-    gather_on(2)
-    hidden(1)
-    hidden_on(0)
     finish(3)
     return_y(1, 0)
+    contrib(2, 0)
     return_y(1, 1)
-    contrib(2, 0)
     gather_on(3)
     contrib(2, 1)
+    return_y(2, 0)
+    contrib(3, 0)
+    hidden(0)
+    hidden(1)
+    return_y(2, 1)
+    contrib(3, 1)
     hidden(2)
     hidden(3)
-    return_y(2, 0)
-    contrib(3, 0)
-    return_y(2, 1)
-    contrib(3, 1)
-    hidden_on(1)
     return_core(0, 0)
     return_core(0, 1)
     return_core(1, 0)
@@ -385,11 +383,13 @@
     combine(0)
     return_y(3, 0)
     return_y(3, 1)
-    hidden_on(2)
-    hidden_on(3)
+    hidden_on(0)
+    hidden_on(1)
     return_core(2, 0)
     return_core(2, 1)
     combine(1)
+    hidden_on(2)
+    hidden_on(3)
     return_core(3, 0)
     return_core(3, 1)
     combine(2)
@@ -419,7 +419,7 @@
 def grads(x_rows, c_rows, hid, bg, bu):
     slots, dq = x_rows.shape
     ff = hid.shape[1]
-    tile = 256
+    tile = dq // 2
     sds = jax.ShapeDtypeStruct
     whole = pl.BlockSpec((slots, ff), lambda i: (0, 0))
     cols = pl.BlockSpec((slots, tile), lambda i: (0, i))

time: 114 us -> 112 us (0.982)
  no operation moved by 1% of the time
where the time goes in v4:
time: 112 us
  Pallas kernels  111 us (99%)
    pallas_call x1, Pallas kernels, local(): pl.pallas_call(body, name='exchange', out_shape=(sds((t_n, dq), BF16), sd...  100 us
    pallas_call x1, Pallas kernels, grads(): pl.pallas_call(grads_body, name='grads', grid=(dq // tile,), out_shape=(s...  10.5 us

profile of v4, /device:TPU:1, one launch (start us, length us, event | category | flops | bytes accessed | tf_op | source)
XLA Modules:
  0.0 112.2 jit_solution(4018995246386149163)
XLA Ops:
  0.6 100.1 %exchange.1 = (bf16[256,1792]{1,0:T(8,128)(2,1)}, bf16[4,4,2,16,1792]{4,3,2,1,0:T(8,128)(2,1)}, bf16[4,4,2,16,1792]{4,3,2,1,0:T(8,128)(2,1)}, bf16[4,4,2,16,1024...) custom-call(bf16[256,1792]{1,0:T(8,128)(2,1)} %tok_h.1, ...), custom_call_target="tpu_custom_call" | custom-call | tf_op jit(solution)/shard_map/exchange/pallas_call | solution.py:452
  100.8 0.0 copy-start
  100.8 10.5 %grads.1 = (bf16[1792,1024]{1,0:T(8,128)(2,1)}, bf16[1792,1024]{1,0:T(8,128)(2,1)}, bf16[1024,1792]{1,0:T(8,128)(2,1)}) custom-call(bf16[512,1792]{1,0:T(8,128)(2,1)} %bitcast.16, bf16[512,1792]{1,0:T(8,128)(2,1)} %bitcast.17, bf16[512,1024]{1,0:T(8,128)(2,1)} %bitcast.18, bf16[512,1024]{1,0:T(8,128)(2,1)} %bitcast.19, bf16[512,1024]{1,0:T(8,128)(2,1)} %bitcast.20), custom_call_target="tpu_custom_call" | custom-call | tf_op jit(solution)/shard_map/grads/pallas_call | solution.py:427
  111.2 0.0 copy-done
  111.2 0.9 copy.12
Async XLA Ops:
  100.8 10.5 %copy-start = (bf16[256,1792]{1,0:T(8,128)(2,1)S(1)}, bf16[256,1792]{1,0:T(8,128)(2,1)}, u32[]{:S(2)}) copy-start(bf16[256,1792]{1,0:T(8,128)(2,1)} %get-tuple-element.26) | copy-start | bytes 2752516
